TPU v7x, 32 devices: a whole 2x2x4 slice. The times are simulated.
32 devices in a mesh: seq: 8 (over z, y), head: 4 (over x, core).
Axes of the slice: x: 2, y: 2, z: 4, core: 2. Of those that a mesh axis runs over, the one named last changes fastest.
Arguments:
- tokens: bfloat16 [4, 2048, 1024], P(None, 'seq'), may hold values from -6 to 6
- norm_gain: float32 [1024], replicated, as said below
- gate_weight: bfloat16 [1024, 2048], P(None, 'head'), may hold values from -0.1875 to 0.1875
- value_weight: bfloat16 [1024, 2048], P(None, 'head'), as said below
- shared_weight: bfloat16 [1024, 256], replicated, may hold values from -0.0234375 to 0.0234375
- step_weight: bfloat16 [1024, 32], P(None, 'head'), may hold values from -0.1875 to 0.1875
- conv_value: float32 [4, 2048], P(None, 'head'), may hold values from -3 to 3
- conv_value_bias: float32 [2048], P('head'), may hold values from -1.8 to 1.8
- conv_shared: float32 [4, 256], replicated, may hold values from -3 to 3
- conv_shared_bias: float32 [256], replicated, may hold values from -0.6 to 0.6
- step_bias: float32 [32], P('head'), may hold values from -1 to 1
- decay_rate: float32 [32], P('head'), as said below
- skip_weight: float32 [32], P('head'), may hold values from 0.5 to 1.5
- out_gain: float32 [2048], P('head'), may hold values from 0.5 to 1.5
- output_weight: bfloat16 [2048, 1024], P('head'), may hold values from -0.125 to 0.125
- cotangent: bfloat16 [4, 2048, 1024], P(None, 'seq', 'head'), may hold values from -6 to 6
Outputs:
- mixed: bfloat16 [4, 2048, 1024], P(None, 'seq', 'head')
- grad_tokens: float32 [4, 2048, 1024], P(None, 'seq', 'head')
- grad_norm_gain: float32 [1024], P('head')
- grad_w_gate: float32 [1024, 2048], P(None, 'head')
- grad_w_value: float32 [1024, 2048], P(None, 'head')
- grad_w_shared: float32 [1024, 256], replicated
- grad_w_step: float32 [1024, 32], P(None, 'head')
- grad_conv_value: float32 [4, 2048], P(None, 'head')
- grad_conv_value_bias: float32 [2048], P('head')
- grad_conv_shared: float32 [4, 256], replicated
- grad_conv_shared_bias: float32 [256], replicated
- grad_step_bias: float32 [32], P('head')
- grad_decay_rate: float32 [32], P('head')
- grad_skip_weight: float32 [32], P('head')
- grad_out_gain: float32 [2048], P('head')
- output_weight_gradient: float32 [2048, 1024], P('head')
Inputs may be any that keep to these rules, and one draw needn't show every extreme that they name: `norm_gain`: gains of the input norm, each between 0.28 and 2.6. Entries of value_weight lie within 10 / sqrt(1024). `decay_rate`: each rate lies between 0.3 / 2048 and 1 / 24.
All inputs are finite; a program needn't handle non-finite values.
Results may differ from a plain program's by a relative error of at most 0.019.
Values may be sent and summed in bfloat16 or wider, within the bound.
A program may use at most 320 MiB of HBM per device.

v0:
```python
import jax
import jax.numpy as jnp
from jax import lax
from jax.sharding import PartitionSpec as P

EPSILON = 1e-05
FULL_PRECISION = lax.Precision.HIGHEST


def shifted(value, axis, steps):
    count = lax.axis_size(axis)
    first, last = (max(0, -steps), min(count, count - steps))
    return lax.ppermute(value, axis, [(source, source + steps) for source in range(first, last)])


def carried_in(shard, axis, join, neutral):
    place = lax.axis_index(axis)
    gathered = jax.tree.map(
        lambda a, kind: lax.all_gather(a.astype(kind), axis), shard, (jnp.bfloat16, jnp.bfloat16)
    )
    state = jax.tree.map(lambda a, e: jnp.zeros_like(a) + jnp.asarray(e, a.dtype), shard, neutral)

    def one(turn, state):
        return join(
            state,
            jax.tree.map(
                lambda a, own: lax.dynamic_index_in_dim(a, turn, 0, False).astype(own.dtype),
                gathered,
                shard,
            ),
        )

    return lax.fori_loop(0, place, one, state)


def carried_in_2(shard, axis, combine, identity):
    count, position = (lax.axis_size(axis), lax.axis_index(axis))
    everything = jax.tree.map(
        lambda part, kind: lax.all_gather(part.astype(kind), axis),
        shard,
        jax.tree.map(lambda a: jnp.bfloat16 if a.dtype == jnp.float32 else a.dtype, shard),
    )
    start = jax.tree.map(
        lambda part, zero: jnp.broadcast_to(jnp.asarray(zero, part.dtype), part.shape),
        shard,
        identity,
    )

    def turn(k, before):
        at = count - 1 - k
        reached = at > position
        new = combine(
            before, jax.tree.map(lambda part, own: part[at].astype(own.dtype), everything, shard)
        )
        return jax.tree.map(lambda a, b: jnp.where(reached, a, b), new, before)

    return lax.fori_loop(0, count, turn, start)


def as_sent(shard):
    return jax.tree.map(lambda a: a.astype(jnp.bfloat16) if a.dtype == jnp.float32 else a, shard)


def silu_act(argument):
    return argument * jax.nn.sigmoid(argument)


def conv_apply(extended, weight_matrix, bias_row):
    taps = weight_matrix.shape[0]
    seq_rows = extended.shape[1] - taps + 1
    running = bias_row + jnp.zeros((extended.shape[0], seq_rows, extended.shape[2]), jnp.float32)
    for offset in range(taps):
        running = running + weight_matrix[offset] * extended[:, offset : offset + seq_rows, :]
    return silu_act(running)


def local_scan(values, keys_state, reads_state, unscaled_step, step_bias, decay_rate, skip_weight):
    steps = jax.nn.softplus(unscaled_step + step_bias)
    logdecay = -steps * decay_rate
    cumulative = jnp.cumsum(logdecay, axis=1)
    scores = jnp.einsum("stn,sun->stu", reads_state, keys_state, precision=FULL_PRECISION)
    block_rows = cumulative.shape[1]
    causal_mask = (
        lax.broadcasted_iota(jnp.int32, (block_rows, block_rows), 0)
        >= lax.broadcasted_iota(jnp.int32, (block_rows, block_rows), 1)
    )[None, None]
    cum_heads = jnp.moveaxis(cumulative, 1, 2)
    log_gaps = cum_heads[:, :, :, None] - cum_heads[:, :, None, :]
    decays = jnp.where(causal_mask, jnp.exp(jnp.where(causal_mask, log_gaps, 0.0)), 0.0)
    weights = decays * scores[:, None] * jnp.moveaxis(steps, 1, 2)[:, :, None, :]
    inner = jnp.einsum("shtu,suhp->sthp", weights, values, precision=FULL_PRECISION)
    local_out = inner + skip_weight[:, None] * values
    tail_weight = jnp.exp(cumulative[:, -1:, :] - cumulative) * steps
    state_part = jnp.einsum(
        "sth,sthp,stn->shpn", tail_weight, values, keys_state, precision=FULL_PRECISION
    )
    return (local_out, state_part, cumulative)


def join_forward(earlier, later):
    return (earlier[0] * later[0], earlier[1] * later[0][:, :, None, None] + later[1])


def join_backward(earlier, later):
    return (earlier[0] * later[0], later[1] + later[0][:, :, None, None] * earlier[1])


def rounded(array):
    return lax.optimization_barrier(array.astype(jnp.bfloat16)).astype(jnp.float32)


def shards(
    tokens,
    norm_gain,
    gate_weight,
    value_weight,
    shared_weight,
    step_weight,
    conv_value,
    conv_value_bias,
    conv_shared,
    conv_shared_bias,
    step_bias,
    decay_rate,
    skip_weight,
    out_gain,
    output_weight,
    cotangent,
):
    batches, seq_rows, model_width = tokens.shape
    inner_dev = gate_weight.shape[1]
    heads_dev = step_weight.shape[1]
    head_size = inner_dev // heads_dev
    state_dim = shared_weight.shape[1] // 2
    slice_width = cotangent.shape[2]
    head_count = lax.axis_size("head")
    offset_head = lax.axis_index("head") * slice_width
    edge_rows = conv_value.shape[0] - 1
    input_rows = tokens.astype(jnp.float32)
    rms_scale = lax.rsqrt(jnp.mean(input_rows * input_rows, axis=-1, keepdims=True) + EPSILON)
    unit_input = input_rows * rms_scale
    normalized = (unit_input * norm_gain).astype(jnp.bfloat16)

    def project(weight_matrix):
        return jnp.einsum(
            "pfn,nv->pfv", normalized, weight_matrix, preferred_element_type=jnp.float32
        )

    gate_projected = project(gate_weight)
    value_projected = project(value_weight)
    shared_projected = project(shared_weight)
    unscaled_step = project(step_weight)
    edge_value, edge_shared = (
        shifted(value_projected[:, seq_rows - edge_rows :].astype(jnp.bfloat16), "seq", 1).astype(
            jnp.float32
        ),
        shifted(shared_projected[:, seq_rows - edge_rows :].astype(jnp.bfloat16), "seq", 1).astype(
            jnp.float32
        ),
    )
    ext_value = jnp.concatenate([edge_value, value_projected], axis=1)
    ext_shared = jnp.concatenate([edge_shared, shared_projected], axis=1)
    conv_out_value, conv_back_value = jax.vjp(conv_apply, ext_value, conv_value, conv_value_bias)
    conv_out_shared, conv_back_shared = jax.vjp(
        conv_apply, ext_shared, conv_shared, conv_shared_bias
    )
    values = rounded(conv_out_value).reshape(batches, seq_rows, heads_dev, head_size)
    mixed_shared = rounded(conv_out_shared)
    keys_state = mixed_shared[:, :, :state_dim]
    reads_state = mixed_shared[:, :, state_dim:]
    (local_out, state_part, cumulative), scan_back = jax.vjp(
        local_scan,
        values,
        keys_state,
        reads_state,
        unscaled_step,
        step_bias,
        decay_rate,
        skip_weight,
    )
    chain_decay = jnp.exp(cumulative[:, -1, :])
    incoming = carried_in(
        (chain_decay, state_part),
        "seq",
        join_forward,
        (jnp.ones_like(chain_decay), jnp.zeros_like(state_part)),
    )
    state_in = incoming[1]
    reaching = jnp.exp(cumulative)[..., None]
    outer = reaching * jnp.einsum("stn,shpn->sthp", reads_state, state_in, precision=FULL_PRECISION)
    ssd_out = (local_out + outer).reshape(batches, seq_rows, inner_dev)
    gate_act = silu_act(gate_projected)
    gated = ssd_out * gate_act
    total_squares = lax.psum(jnp.sum(gated * gated, axis=-1), "head")
    gate_scale = lax.rsqrt(total_squares / (inner_dev * head_count) + EPSILON)[..., None]
    gate_unit = gated * gate_scale
    normalized_output = (gate_unit * out_gain).astype(jnp.bfloat16)
    partial_output = jnp.einsum(
        "ufc,cq->ufq", normalized_output, output_weight, preferred_element_type=jnp.float32
    )
    branch_out = lax.psum_scatter(
        partial_output.astype(jnp.bfloat16), "head", scatter_dimension=2, tiled=True
    ).astype(jnp.float32)
    own_unit = lax.dynamic_slice_in_dim(unit_input, offset_head, slice_width, 2)
    own_inputs = lax.dynamic_slice_in_dim(input_rows, offset_head, slice_width, 2)
    mixed = (own_inputs + branch_out).astype(jnp.bfloat16)
    complete_cotangent = lax.all_gather(cotangent, "head", axis=2, tiled=True)
    output_weight_gradient = jnp.einsum(
        "bwz,bwu->zu", normalized_output, complete_cotangent, preferred_element_type=jnp.float32
    )
    normalized_output_gradient = jnp.einsum(
        "buz,gz->bug", complete_cotangent, output_weight, preferred_element_type=jnp.float32
    )
    grad_out_gain = jnp.sum(normalized_output_gradient * gate_unit, axis=(0, 1))
    d_unit_y = normalized_output_gradient * out_gain
    dot_total = lax.psum(jnp.sum(d_unit_y * gate_unit, axis=-1), "head")
    d_gated = gate_scale * (
        d_unit_y - gate_unit * (dot_total / (inner_dev * head_count))[..., None]
    )
    d_ssd = (d_gated * gate_act).reshape(batches, seq_rows, heads_dev, head_size)
    gate_sigmoid = jax.nn.sigmoid(gate_projected)
    d_gate = d_gated * ssd_out * gate_sigmoid * (1.0 + gate_projected * (1.0 - gate_sigmoid))
    weighted = d_ssd * reaching
    direct = jnp.einsum("sthp,stn->shpn", weighted, reads_state, precision=FULL_PRECISION)
    carried = carried_in_2(
        (chain_decay, direct),
        "seq",
        join_backward,
        (jnp.ones_like(chain_decay), jnp.zeros_like(direct)),
    )
    grad_state_out = carried[1]
    d_reads_outer = jnp.einsum("sthp,shpn->stn", weighted, state_in, precision=FULL_PRECISION)
    d_cumulative = jnp.sum(d_ssd * outer, axis=-1)
    end_term = jnp.sum(grad_state_out * state_in, axis=(2, 3)) * chain_decay
    d_cumulative = d_cumulative.at[:, -1, :].add(end_term)
    d_values, d_keys, d_reads, d_raw_step, grad_step_bias, grad_decay_rate, grad_skip_weight = (
        scan_back((d_ssd, grad_state_out, d_cumulative))
    )
    d_mixed_shared = jnp.concatenate([d_keys, d_reads + d_reads_outer], axis=-1)
    d_ext_value, grad_conv_value, grad_conv_value_bias = conv_back_value(
        d_values.reshape(batches, seq_rows, inner_dev)
    )
    d_ext_shared, grad_conv_shared, grad_conv_shared_bias = conv_back_shared(d_mixed_shared)
    back_value, back_shared = shifted(
        (as_sent(d_ext_value[:, :edge_rows]), as_sent(d_ext_shared[:, :edge_rows])), "seq", -1
    )
    d_value = d_ext_value[:, edge_rows:].at[:, seq_rows - edge_rows :].add(back_value)
    d_shared = d_ext_shared[:, edge_rows:].at[:, seq_rows - edge_rows :].add(back_shared)
    d_gate_low = d_gate.astype(jnp.bfloat16)
    d_value_low = d_value.astype(jnp.bfloat16)
    d_shared_low = d_shared.astype(jnp.bfloat16)
    d_step_low = d_raw_step.astype(jnp.bfloat16)

    def weight_grad(gradient_result):
        return jnp.einsum(
            "org,orj->gj", normalized, gradient_result, preferred_element_type=jnp.float32
        )

    def back_project(gradient_result, weight_matrix):
        return jnp.einsum(
            "tuf,kf->tuk", gradient_result, weight_matrix, preferred_element_type=jnp.float32
        )

    grad_w_gate = weight_grad(d_gate_low)
    grad_w_value = weight_grad(d_value_low)
    grad_w_shared = weight_grad(d_shared_low)
    grad_w_step = weight_grad(d_step_low)
    d_normed = (
        back_project(d_gate_low, gate_weight)
        + back_project(d_value_low, value_weight)
        + back_project(d_shared_low, shared_weight)
        + back_project(d_step_low, step_weight)
    )
    own_gain = lax.dynamic_slice_in_dim(norm_gain, offset_head, slice_width, 0)
    d_own = lax.psum_scatter(
        d_normed.astype(jnp.bfloat16), "head", scatter_dimension=2, tiled=True
    ).astype(jnp.float32)
    d_unit = d_own * own_gain
    row_dot = lax.psum(jnp.sum(d_unit * own_unit, axis=-1), "head")
    grad_norm_gain = jnp.sum(d_own * own_unit, axis=(0, 1))
    grad_tokens = cotangent.astype(jnp.float32) + rms_scale * (
        d_unit - own_unit * (row_dot / model_width)[..., None]
    )
    head_grads = (
        grad_w_gate,
        grad_w_value,
        grad_w_step,
        grad_conv_value,
        grad_conv_value_bias,
        grad_step_bias,
        grad_decay_rate,
        grad_skip_weight,
        grad_out_gain,
        grad_norm_gain,
    )
    pending = head_grads + (output_weight_gradient,)
    summed = lax.psum(pending, "seq")
    output_weight_gradient = summed[10]
    grad_w_shared, grad_conv_shared, grad_conv_shared_bias = lax.psum(
        (grad_w_shared, grad_conv_shared, grad_conv_shared_bias), ("seq", "head")
    )
    return (
        mixed,
        grad_tokens,
        summed[9],
        summed[0],
        summed[1],
        grad_w_shared,
        summed[2],
        summed[3],
        summed[4],
        grad_conv_shared,
        grad_conv_shared_bias,
        summed[5],
        summed[6],
        summed[7],
        summed[8],
        output_weight_gradient,
    )


def solution(mesh):
    return jax.shard_map(
        shards,
        mesh=mesh,
        in_specs=(
            P(None, "seq", None),
            P(),
            P(None, "head"),
            P(None, "head"),
            P(),
            P(None, "head"),
            P(None, "head"),
            P("head"),
            P(),
            P(),
            P("head"),
            P("head"),
            P("head"),
            P("head"),
            P("head", None),
            P(None, "seq", "head"),
        ),
        out_specs=(
            P(None, "seq", "head"),
            P(None, "seq", "head"),
            P("head"),
            P(None, "head"),
            P(None, "head"),
            P(),
            P(None, "head"),
            P(None, "head"),
            P("head"),
            P(),
            P(),
            P("head"),
            P("head"),
            P("head"),
            P("head"),
            P("head", None),
        ),
        check_vma=False,
    )
```

profile of v0, /device:TPU:0, one launch (start us, length us, event | category | flops | bytes accessed | tf_op | source)
XLA Modules:
  0.0 722.8 jit_solution(14170734373520905780)
XLA Ops:
  12.2 5.0 collective-permute-start
  39.5 26.3 %all-gather = bf16[32,1,8]{2,1,0:T(2,128)(2,1)S(1)} all-gather(bf16[4,1,8]{2,1,0:T(2,128)(2,1)S(1)} %copy.174), channel_id=2, replica_groups=mesh['seq'=8,'head'=4] {'seq'}, dimensions={0}, use_global_device_ids=true | all-gather | bytes 576 | tf_op jit(solution)/shard_map/all_gather | solution.py:19
  71.5 41.2 %all-gather.9.cloned.1.call-done = bf16[32,8,64,128]{3,2,1,0:T(8,128)(2,1)} async-done(((bf16[4,8,64,128]{3,2,1,0:T(8,128)(2,1)}), bf16[32,8,64,128]{3,2,1,0:T(8,128)(2,1)}) %all-gather.9.cloned.1.call-update) | async-done | bytes 4194320 | tf_op jit(solution)/shard_map/all_gather | solution.py:19
  115.2 9.2 %fusion.29 = f32[4,256,8,64]{1,3,2,0:T(8,128)} fusion(f32[4,256,8,64]{1,3,2,0:T(8,128)S(1)} %bitcast.210, f32[4,256,8,64]{1,3,2,0:T(8,128)S(1)} %fusion.91, bf16[4,256,8,64]{1,3,2,0:T(8,128)(2,1)S(1)} %bitcast.209, f32[4,8,256]{2,1,0:T(8,128)S(1)} %copy.171, f32[4,256,256]{2,1,0:T(8,128)} %fusion.101, f32[4,8,256]{2,1,0:T(8,128)S(1)} %copy.169, ...), kind=kOutput, calls=%fused_computation.47 | convolution fusion | flops 1623195648 | bytes 8552480 | tf_op jit(solution)/shard_map/jvp(shtu,suhp->sthp)/dot_general | solution.py:91
  127.3 5.8 multiply_reduce_fusion.11
  133.1 5.6 psum.119
  138.7 5.9 multiply_reduce_fusion.3
  144.6 6.6 psum.120
  151.3 6.0 multiply_reduce_fusion.4
  168.0 12.1 %fusion.9 = (f32[4,8,256]{2,1,0:T(8,128)S(1)}, f32[4,8,256]{2,1,0:T(8,128)S(1)}, f32[4,8,256]{2,1,0:T(8,128)S(1)}, f32[4,256,256]{2,1,0:T(8,128)}) fusion(f32[4,8,256]{2,1,0:T(8,128)S(1)} %copy.171, f32[4,256,256]{2,1,0:T(8,128)} %fusion.101, f32[4,8,256]{2,1,0:T(8,128)S(1)} %copy.169, pred[256,256]{1,0:T(8,128)(4,1)S(1)} %iota_compare_fusion, ...), kind=kOutput, calls=%fused_computation.15 | convolution fusion | flops 1641783296 | bytes 5472256 | tf_op jit(solution)/shard_map/transpose(jvp(shtu,suhp->sthp))/dot_general | solution.py:91
  183.1 5.2 fusion.46
  197.5 47.2 %all-gather.11.cloned.1.call-done = bf16[32,8,64,128]{3,2,1,0:T(8,128)(2,1)} async-done(((bf16[4,8,64,128]{3,2,1,0:T(8,128)(2,1)}), bf16[32,8,64,128]{3,2,1,0:T(8,128)(2,1)}) %all-gather.11.cloned.1.call-update) | async-done | bytes 4194320 | tf_op jit(solution)/shard_map/all_gather | solution.py:39
  244.6 10.9 %while.32 = (s32[]{:T(128)}, f32[4,8,64,128]{3,2,1,0:T(8,128)S(1)}, s32[]{:T(128)}, bf16[8,4,8,64,128]{4,3,2,1,0:T(8,128)(2,1)}, bf16[8,4,8]{2,1,0:T(4,128)(2,1)...) while((s32[]{:T(128)}, f32[4,8,64,128]{3,2,1,0:T(8,128)S(1)}, s32[]{:T(128)}, ...), condition=%wide.region_11.12_spmd.clone, body=%wide.region_10.11_spmd.clone.sunk | while | flops 1310760 | bytes 2621927 | solution.py:57
  255.5 4.8 fusion.45
  263.5 8.8 %bitcast_add_fusion = f32[4,256,8,64]{1,3,2,0:T(8,128)} fusion(f32[4,256,8,64]{1,3,2,0:T(8,128)S(1)} %bitcast.201, f32[4,256,8,64]{1,3,2,0:T(8,128)S(1)} %get-tuple-element.340, f32[4,8,64,256]{3,2,1,0:T(8,128)S(1)} %bitcast.202, f32[4,8,256]{2,1,0:T(8,128)S(1)} %copy.171, f32[4,256,256]{2,1,0:T(8,128)S(1)} %copy-done.47, f32[4,8,256]{2,1,0:T(8,128)S(1)} %copy.169, ...), kind=kOutput, calls=%fused_computation.45 | convolution fusion | flops 1623195648 | bytes 9601056 | tf_op jit(solution)/shard_map/transpose(jvp(shtu,suhp->sthp))/dot_general | solution.py:91
  275.2 5.7 multiply_reduce_fusion.7
  292.7 9.9 %reduce-window.16 = f32[4,8,2,128]{3,1,2,0:T(8,128)S(1)} reduce-window(f32[4,8,2,128]{3,1,2,0:T(8,128)S(1)} %copy.192, f32[]{:T(128)} %constant.171.clone.1), window={size=1x1x1x128 pad=0_0x0_0x0_0x0_127}, to_apply=%region_19.20 | reduce-window | flops 1040384 | bytes 65540 | tf_op jit(solution)/shard_map/reduce-window.2
  314.9 4.6 add_convert_fusion
  326.2 5.3 convolution_bitcast_fusion
  341.8 42.9 %all-reduce.17 = (f32[4,256]{1,0:T(4,128)}, f32[256]{0:T(256)}) all-reduce(f32[4,256]{1,0:T(4,128)S(1)} %pad_add_fusion.3, f32[256]{0:T(256)S(1)} %get-tuple-element.265), channel_id=1, replica_groups=mesh['seq'=8,'head'=4] {'seq','head'}, use_global_device_ids=true, to_apply=%region_41.42 | all-reduce | flops 1280 | bytes 10240 | tf_op jit(solution)/shard_map/psum | solution.py:299
  387.1 37.8 %all-reduce.18 = (f32[256]{0:T(256)}, f32[1024,8]{0,1:T(8,128)}, f32[4,512]{1,0:T(4,128)}, f32[512]{0:T(512)}, f32[8]{0:T(128)}, /*index=5*/f32[8]{0:T(128)}, f32[8]{0:T(128)}, f32[512]{0:T(512)}) all-reduce(f32[256]{0:T(256)S(1)} %get-tuple-element.252, ...), channel_id=1, replica_groups=mesh['seq'=8,'head'=4] {'seq'}, use_global_device_ids=true, to_apply=%region_25.26 | all-reduce | flops 11544 | bytes 92352 | tf_op jit(solution)/shard_map/psum | solution.py:297
  424.9 5.7 psum.121
  433.3 55.7 %all-reduce.23.cloned.1.call-done = f32[1024,256]{1,0:T(8,128)} async-done(((f32[1024,256]{1,0:T(8,128)}), f32[1024,256]{1,0:T(8,128)}) %all-reduce.23.cloned.1.call-update) | async-done | bytes 1048592 | tf_op jit(solution)/shard_map/psum | solution.py:299
  489.1 218.0 %all-reduce.25.cloned.1.call-done = (f32[1024,512]{1,0:T(8,128)}, f32[1024,512]{1,0:T(8,128)}, f32[512,1024]{1,0:T(8,128)}) async-done(((f32[1024,512]{1,0:T(8,128)}, f32[1024,512]{1,0:T(8,128)}, f32[512,1024]{1,0:T(8,128)}), (f32[1024,512]{1,0:T(8,128)}, f32[1024,512]{1,0:T(8,128)}, f32[512,1024]{1,0:T(8,128)})) %all-reduce.25.cloned.1.call-update) | async-done | bytes 6291472 | tf_op jit(solution)/shard_map/psum | solution.py:297
  (287 shorter events, 131.6 us)
Async XLA Ops:
  7.2 120.1 %copy-start = (bf16[1024,512]{1,0:T(8,128)(2,1)S(1)}, bf16[1024,512]{1,0:T(8,128)(2,1)}, u32[]{:S(2)}) copy-start(bf16[1024,512]{1,0:T(8,128)(2,1)} %param.28) | copy-start | bytes 3145732
  7.2 105.4 %all-gather.9.cloned.1.call-start = ((), (), s32[]{:S(2)}) async-start(), calls=%async_computation.6 | async-start | bytes 4718592 | tf_op jit(solution)/shard_map/all_gather | solution.py:19
  9.5 7.7 %copy-start.49 = (bf16[1024,256]{1,0:T(8,128)(2,1)S(1)}, bf16[1024,256]{1,0:T(8,128)(2,1)}, u32[]{:S(2)}) copy-start(bf16[1024,256]{1,0:T(8,128)(2,1)} %param.30) | copy-start | bytes 1572868
  12.1 9.4 %copy-start.51 = (bf16[1024,8]{0,1:T(8,128)(2,1)S(1)}, bf16[1024,8]{0,1:T(8,128)(2,1)}, u32[]{:S(2)}) copy-start(bf16[1024,8]{0,1:T(8,128)(2,1)} %param.31) | copy-start | bytes 49156
  12.2 19.6 %collective-permute-start = (bf16[4,3,512]{2,1,0:T(4,128)(2,1)S(1)}, bf16[4,3,512]{2,1,0:T(4,128)(2,1)S(1)}, u32[]{:S(2)}, u32[]{:S(2)}) collective-permute-start(bf16[4,3,512]{2,1,0:T(4,128)(2,1)S(1)} %slice.300), channel_id=1, source_target_pairs={{0,4},{4,8},{8,12},{12,16},{16,20},{20,24},{24,28},{1,5},{5,9},{9,... | collective-permute-start | bytes 36872 | tf_op jit(solution)/shard_map/ppermute | solution.py:13
  18.0 12.1 %collective-permute-start.1 = (bf16[4,3,256]{2,1,0:T(4,128)(2,1)S(1)}, bf16[4,3,256]{2,1,0:T(4,128)(2,1)S(1)}, u32[]{:S(2)}, u32[]{:S(2)}) collective-permute-start(bf16[4,3,256]{2,1,0:T(4,128)(2,1)S(1)} %slice.302), channel_id=1, source_target_pairs={{0,4},{4,8},{8,12},{12,16},{16,20},{20,24},{24,28},{1,5},{5,9},{9,... | collective-permute-start | bytes 18440 | tf_op jit(solution)/shard_map/ppermute | solution.py:13
  22.6 6.2 copy-start.8
  27.1 40.0 %copy-start.6 = (f32[4,8,2,128]{1,0,3,2:T(4,128)}, f32[4,8,2,128]{1,0,3,2:T(4,128)S(1)}, u32[]{:S(2)}) copy-start(f32[4,8,2,128]{1,0,3,2:T(4,128)S(1)} %copy.168) | copy-start | bytes 98308
  31.8 36.7 %copy-start.10 = (bf16[4,256,256]{2,1,0:T(8,128)(2,1)}, bf16[4,256,256]{2,1,0:T(8,128)(2,1)S(1)}, u32[]{:S(2)}) copy-start(bf16[4,256,256]{2,1,0:T(8,128)(2,1)S(1)} %get-tuple-element.309) | copy-start | bytes 1572868
  38.7 100.0 %all-gather.7.cloned.1.call-start = ((), (), s32[]{:S(2)}) async-start(), calls=%async_computation.3 | async-start | bytes 2621440 | tf_op jit(solution)/shard_map/all_gather | solution.py:207
  39.4 205.2 %all-gather.11.cloned.1.call-start = ((), (), s32[]{:S(2)}) async-start(), calls=%async_computation.7 | async-start | bytes 4718592 | tf_op jit(solution)/shard_map/all_gather | solution.py:39
  115.1 9.2 %copy-start.18 = (f32[4,256,8,64]{1,3,2,0:T(8,128)}, f32[4,256,8,64]{1,3,2,0:T(8,128)S(1)}, u32[]{:S(2)}) copy-start(f32[4,256,8,64]{1,3,2,0:T(8,128)S(1)} %fusion.91) | copy-start | bytes 6291460
  127.3 11.5 %copy-start.60 = (f32[512]{0:T(512)S(1)}, f32[512]{0:T(512)}, u32[]{:S(2)}) copy-start(f32[512]{0:T(512)} %param.39) | copy-start | bytes 6148
  163.7 175.7 %reduce-scatter.3.cloned.1.call-start = ((), (), s32[]{:S(2)}) async-start(), calls=%async_computation.2 | async-start | bytes 2621440 | tf_op jit(solution)/shard_map/reduce_scatter | solution.py:201
  183.1 6.7 copy-start.68
  197.2 188.1 %reduce-scatter.5.cloned.1.call-start = ((), (), s32[]{:S(2)}) async-start(), calls=%async_computation.4 | async-start | bytes 2621440 | tf_op jit(solution)/shard_map/reduce_scatter | solution.py:275
  283.4 27.6 %collective-permute-start.2 = (bf16[4,3,512]{2,1,0:T(4,128)(2,1)S(1)}, bf16[4,3,512]{2,1,0:T(4,128)(2,1)S(1)}, u32[]{:S(2)}, u32[]{:S(2)}) collective-permute-start(bf16[4,3,512]{2,1,0:T(4,128)(2,1)S(1)} %slice.299), channel_id=1, source_target_pairs={{4,0},{8,4},{12,8},{16,12},{20,16},{24,20},{28,24},{5,1},{9,5},{13... | collective-permute-start | bytes 36872 | tf_op jit(solution)/shard_map/ppermute | solution.py:13
  287.7 22.0 %collective-permute-start.3 = (bf16[4,3,256]{2,1,0:T(4,128)(2,1)S(1)}, bf16[4,3,256]{2,1,0:T(4,128)(2,1)S(1)}, u32[]{:S(2)}, u32[]{:S(2)}) collective-permute-start(bf16[4,3,256]{2,1,0:T(4,128)(2,1)S(1)} %slice.301), channel_id=1, source_target_pairs={{4,0},{8,4},{12,8},{16,12},{20,16},{24,20},{28,24},{5,1},{9,5},{13... | collective-permute-start | bytes 18440 | tf_op jit(solution)/shard_map/ppermute | solution.py:13
  292.2 10.9 %copy-start.22 = (f32[4,256,8]{2,0,1:T(4,128)S(1)}, f32[4,256,8]{2,0,1:T(4,128)}, u32[]{:S(2)}) copy-start(f32[4,256,8]{2,0,1:T(4,128)} %copy.214) | copy-start | bytes 98308
  292.2 10.9 %copy-start.42 = (f32[4,8,256]{1,0,2:T(4,128)S(1)}, f32[4,8,256]{1,0,2:T(4,128)}, u32[]{:S(2)}) copy-start(f32[4,8,256]{1,0,2:T(4,128)} %copy.187) | copy-start | bytes 98308
  292.2 10.9 %copy-start.64 = (f32[8]{0:T(128)S(1)}, f32[8]{0:T(128)}, u32[]{:S(2)}) copy-start(f32[8]{0:T(128)} %param.37) | copy-start | bytes 100
  319.6 169.5 %all-reduce.23.cloned.1.call-start = ((), (), s32[]{:S(2)}) async-start(), calls=%async_computation.5 | async-start | bytes 2097152 | tf_op jit(solution)/shard_map/psum | solution.py:299
  325.9 381.1 %all-reduce.25.cloned.1.call-start = ((), (), s32[]{:S(2)}) async-start(), calls=%async_computation.8 | async-start | bytes 12582912 | tf_op jit(solution)/shard_map/psum | solution.py:297
  384.7 45.9 %copy-start.36 = (bf16[4,256,256]{2,1,0:T(8,128)(2,1)S(1)}, bf16[4,256,256]{2,1,0:T(8,128)(2,1)}, u32[]{:S(2)}) copy-start(bf16[4,256,256]{2,1,0:T(8,128)(2,1)} %param.41) | copy-start | bytes 1572868
  (58 other events, 175.0 us)
Sparse Core Ops, SparseCore 0:
  38.8 73.7 all-gather.8
  114.2 21.0 all-gather.6
  163.8 80.7 all-gather.10
  247.0 29.6 reduce-scatter.2
  319.7 33.9 reduce-scatter.4
  358.8 130.2 all-reduce.22
  494.5 212.4 all-reduce.24
where the time goes:
time: 732 us; the launch traced here: 723 us
  waiting for transfers between devices  363 us (50%)
  blocking collectives  125 us (17%)
  matrix products  101 us (14%)
  other arithmetic  65.6 us (9%)
  local copies, waits for them, and re-layouts  39.5 us (5%)
  between operations  15.5 us (2%)
  starting transfers between devices  12.6 us (2%)
    psum x1, waiting for transfers between devices, shards(): summed = lax.psum(pending, 'seq')  218 us
    psum x1, waiting for transfers between devices, shards(): lax.psum((grad_w_shared, grad_conv_shared, grad_conv_shared_bias), ('seq'...  55.7 us
    all_gather x1, waiting for transfers between devices, carried_in_2(): lax.all_gather(part.astype(kind), axis)  47.2 us
    psum x1, blocking collectives, shards(): lax.psum((grad_w_shared, grad_conv_shared, grad_conv_shared_bias), ('seq'...  42.9 us
    all_gather x1, waiting for transfers between devices, carried_in(): lax.all_gather(a.astype(kind), axis)  41.2 us
    psum x1, blocking collectives, shards(): summed = lax.psum(pending, 'seq')  37.8 us
    dot_general x3, matrix products, local_scan(): jnp.einsum('shtu,suhp->sthp', weights, values, precision=FULL_PRECISION)  30.1 us
    all_gather x1, blocking collectives, carried_in(): lax.all_gather(a.astype(kind), axis)  26.3 us
  transfers between devices with their start and end apart: 11, of which 4 were waited for; matrix products, arithmetic and copies ran while one was open for 22% of the time, Pallas kernels for 0%

commit v1 on v0

v1 whole, which is shorter than its diff:
```python
import jax
import jax.numpy as jnp
from jax import lax
from jax.experimental import pallas as pl
from jax.experimental.pallas import tpu as pltpu
from jax.sharding import PartitionSpec as P

EPSILON = 1e-05
F32 = jnp.float32
BF = jnp.bfloat16
MESH = pl.DeviceIdType.MESH
LANES = 128


def mm(a, b):
    return lax.dot_general(a, b, (((1,), (0,)), ((), ())), preferred_element_type=F32)


def nt(a, b):
    return lax.dot_general(a, b, (((1,), (1,)), ((), ())), preferred_element_type=F32)


def tn(a, b):
    return lax.dot_general(a, b, (((0,), (0,)), ((), ())), preferred_element_type=F32)


def split(x):
    high = x.astype(BF)
    return high, (x - high.astype(F32)).astype(BF)


def mm_exact_left(a, x):
    high, rest = x.astype(BF), x - x.astype(BF).astype(F32)
    mid, low = split(rest)
    return mm(a, high) + (mm(a, mid) + mm(a, low))


def sigmoid(x):
    return 1.0 / (1.0 + jnp.exp(-x))


def loop(count, body):
    def step(i, carry):
        body(i)
        return carry

    lax.fori_loop(0, count, step, 0)


class Reduced:
    def __init__(self, buf, base, rows, inbox, inbase, levels, sems, first):
        self.buf, self.inbox, self.levels = buf, inbox, levels
        self.send, self.recv, self.free = sems
        self.first = first
        self.lo, self.size, self.stack, self.offset = base, rows, [], inbase
        self.copies = {}

    def copy(self, src, dst, slot, partner):
        return pltpu.make_async_remote_copy(
            src_ref=src,
            dst_ref=dst,
            send_sem=self.send.at[slot],
            recv_sem=self.recv.at[slot],
            device_id=partner,
            device_id_type=MESH,
        )

    def start(self, level):
        partner, bit = self.levels[level]
        halved = self.size // 2 >= 16
        part = self.size // 2 if halved else self.size
        theirs = self.lo + (1 - bit) * part if halved else self.lo
        mine = self.lo + bit * part if halved else self.lo
        copy = self.copy(
            self.buf.at[pl.ds(pl.multiple_of(theirs, 16), part), :],
            self.inbox.at[pl.ds(self.offset, part), :],
            self.first + level,
            partner,
        )
        copy.start()
        self.copies[level] = (copy, mine, part, self.offset, halved)
        self.offset += part

    def finish(self, level):
        copy, mine, part, offset, halved = self.copies[level]
        copy.wait()
        if halved:
            pl.semaphore_signal(
                self.free.at[self.first + level],
                inc=1,
                device_id=self.levels[level][0],
                device_id_type=MESH,
            )
        block = min(part, 64)

        def add(i):
            rows = pl.ds(pl.multiple_of(mine + i * block, 16), block)
            got = self.inbox[pl.ds(pl.multiple_of(offset + i * block, 16), block), :]
            self.buf[rows, :] = (self.buf[rows, :].astype(F32) + got.astype(F32)).astype(BF)

        loop(part // block, add)
        self.stack.append((self.lo, self.size, halved))
        self.lo, self.size = mine, part

    def spread_start(self, level):
        slot = self.first + len(self.levels) + level
        rows = pl.ds(pl.multiple_of(self.lo, 16), self.size)
        pl.semaphore_wait(self.free.at[self.first + level], 1)
        self.copies[level] = self.copy(self.buf.at[rows, :], self.buf.at[rows, :], slot, self.levels[level][0])
        self.copies[level].start()

    def steps(self):
        count = len(self.levels)
        for level in range(count):
            self.start(level)
            yield
            self.finish(level)
        for level in range(count - 1, -1, -1):
            lo, size, halved = self.stack[level]
            if halved:
                self.spread_start(level)
                yield
                self.copies[level].wait()
            self.lo, self.size = lo, size


def kernel(dims, *refs):
    n, S, T, D, C, H, N, F = dims
    PW = C // H
    Sh = S // 2
    R = Sh * C // n
    q = n // Sh
    groups = max(1, R // PW)
    span = R // groups
    names = dims_names(dims)
    ref = dict(zip(names, refs))

    class A:
        pass

    a = A()
    a.__dict__.update(ref)
    me = lax.axis_index("seq")
    head = lax.axis_index("head")
    flip = lambda value, bit: value + bit - 2 * bit * lax.rem(value // bit, 2)
    core_peer = (me, flip(head, 1))
    x_peer = (me, flip(head, 2))
    diag = (me, flip(flip(head, 1), 2))
    barrier = pltpu.get_barrier_semaphore()
    for peer in (core_peer, x_peer, diag):
        pl.semaphore_signal(barrier, inc=1, device_id=peer, device_id_type=MESH)

    def greet(i):
        peer = (lax.rem(me + i + 1, n), head)
        pl.semaphore_signal(barrier, inc=1, device_id=peer, device_id_type=MESH)

    loop(n - 1, greet)

    lane = lax.broadcasted_iota(jnp.int32, (T, LANES), 1)
    first_half = lane < PW

    rows_i = lax.broadcasted_iota(jnp.int32, (T, T), 0)
    cols_i = lax.broadcasted_iota(jnp.int32, (T, T), 1)
    a.tri[...] = jnp.where(rows_i >= cols_i, 1.0, 0.0).astype(BF)
    a.triT[...] = jnp.where(rows_i <= cols_i, 1.0, 0.0).astype(BF)
    er = lax.broadcasted_iota(jnp.int32, (2 * LANES, C), 0)
    ec_ = lax.broadcasted_iota(jnp.int32, (2 * LANES, C), 1)
    a.E2[...] = jnp.where(lax.rem(er, LANES) == ec_ // PW, 1.0, 0.0).astype(BF)
    tr = lax.broadcasted_iota(jnp.int32, (C, LANES), 0)
    tc = lax.broadcasted_iota(jnp.int32, (C, LANES), 1)
    a.ET[...] = jnp.where(tr // PW == tc, 1.0, 0.0).astype(BF)
    a.stT[...] = jnp.zeros(a.stT.shape, BF)
    a.stT[0:H, :] = a.step_weight[...]
    a.small[...] = jnp.zeros(a.small.shape, F32)
    a.heads_sm[...] = jnp.zeros(a.heads_sm.shape, F32)
    a.shsm[...] = jnp.zeros(a.shsm.shape, F32)
    a.hrow[...] = jnp.zeros(a.hrow.shape, F32)
    a.hrow[0:1, 0:H] = a.step_bias[...]
    a.hrow[1:2, 0:H] = a.decay_rate[...]
    a.hrow[2:3, 0:H] = a.skip_weight[...]
    bias_row = a.hrow[0:1, :]
    rate_row = a.hrow[1:2, :]

    def expand(x):
        high, low = split(x)
        return mm(jnp.concatenate([high, low], axis=1), a.E2[...])

    a.skipE[...] = expand(jnp.broadcast_to(a.hrow[2:3, :], (8, LANES)))
    skip_row = a.skipE[0:1, :]
    gain = a.norm_gain[...]

    def norm_rows(x):
        scale = lax.rsqrt(jnp.mean(x * x, axis=-1, keepdims=True) + EPSILON)
        return (x * scale * gain).astype(BF), scale

    def norm_block(b):
        s, r = b // 4, pl.multiple_of(lax.rem(b, 4) * (T // 4), T // 4)
        rows = pl.ds(r, T // 4)
        x = a.tokens[s, rows, :].astype(F32)
        low, scale = norm_rows(x)
        a.normed[s, rows, :] = low
        a.rms[s, rows, :] = jnp.broadcast_to(scale, (T // 4, LANES))

    pl.semaphore_wait(barrier, n - 1 + 3)

    def halo_copy():
        return pltpu.make_async_remote_copy(
            src_ref=a.tokens.at[:, pl.ds(T - 16, 16), :],
            dst_ref=a.halo,
            send_sem=a.ssem.at[0],
            recv_sem=a.rsem.at[0],
            device_id=(lax.rem(me + 1, n), head),
            device_id_type=MESH,
        )

    @pl.when(me < n - 1)
    def _():
        halo_copy().start()

    def cot_copy(src, slot, sem, peer):
        return pltpu.make_async_remote_copy(
            src_ref=src,
            dst_ref=a.cotf.at[slot],
            send_sem=a.ssem.at[sem],
            recv_sem=a.rsem.at[sem],
            device_id=peer,
            device_id_type=MESH,
        )

    cot_x = cot_copy(a.cotangent, head, 1, x_peer)
    cot_x.start()
    cot_c = cot_copy(a.cotangent, head, 2, core_peer)
    cot_c.start()
    cot_own = pltpu.make_async_copy(a.cotangent, a.cotf.at[head], a.lsem.at[0])
    cot_own.start()

    def half(which, f):
        loop(Sh, lambda i: f(which * Sh + i))

    loop(4 * Sh, norm_block)

    def project_b(s):
        x = a.normed[s]
        a.vext[s, 8 : 8 + T, :] = mm(x, a.value_weight[...])
        a.sext[s, 8 : 8 + T, :] = mm(x, a.shared_weight[...])
        a.raw[s] = nt(x, a.stT[...]) + bias_row

    half(0, project_b)

    @pl.when(me > 0)
    def _():
        halo_copy().wait_recv()

    @pl.when(me == 0)
    def _():
        a.halo[...] = jnp.zeros(a.halo.shape, BF)

    @pl.when(me < n - 1)
    def _():
        halo_copy().wait_send()

    hx = jnp.concatenate([a.halo[s] for s in range(S)], axis=0).astype(F32)
    hlow, _ = norm_rows(hx)
    vh = mm(hlow, a.value_weight[...])
    sh = mm(hlow, a.shared_weight[...])
    for s in range(S):
        a.vext[s, 0:8, :] = vh[s * 16 + 8 : s * 16 + 16, :]
        a.sext[s, 0:8, :] = sh[s * 16 + 8 : s * 16 + 16, :]

    def conv(ext, w, b, s, c):
        running = b[0:1, c : c + LANES] + jnp.zeros((T, LANES), F32)
        for k in range(4):
            running = running + w[k : k + 1, c : c + LANES] * ext[s, pl.ds(5 + k, T), c : c + LANES]
        sig = sigmoid(running)
        return running * sig, sig * (1.0 + running * (1.0 - sig))

    def states(tag, reverse):
        m1, o2 = a.__dict__["m1" + tag[1]], a.__dict__["o2" + tag[1]]
        i1, i2 = (a.__dict__[k + tag] for k in ("i1", "i2"))
        s1, r1, s2, r2 = (a.__dict__[k + tag] for k in ("s1", "r1", "s2", "r2"))

        def first(k):
            return pltpu.make_async_remote_copy(
                src_ref=m1.at[k],
                dst_ref=i1.at[me],
                send_sem=s1.at[k],
                recv_sem=r1.at[me],
                device_id=(k, head),
                device_id_type=MESH,
            )

        def first_wait(k):
            return pltpu.make_async_remote_copy(
                src_ref=m1.at[k],
                dst_ref=i1.at[k],
                send_sem=s1.at[k],
                recv_sem=r1.at[k],
                device_id=(k, head),
                device_id_type=MESH,
            )

        def second(k):
            return pltpu.make_async_remote_copy(
                src_ref=o2.at[k],
                dst_ref=i2.at[me],
                send_sem=s2.at[k],
                recv_sem=r2.at[me],
                device_id=(k, head),
                device_id_type=MESH,
            )

        def second_wait(k):
            return pltpu.make_async_remote_copy(
                src_ref=o2.at[k],
                dst_ref=i2.at[k],
                send_sem=s2.at[k],
                recv_sem=r2.at[k],
                device_id=(k, head),
                device_id_type=MESH,
            )

        none = n - 1 if reverse else 0

        def pack(i, state, decay):
            high, low = split(decay)
            hf, lf = high.astype(F32), low.astype(F32)
            for j in range(q):
                h0 = j * R // PW
                k = i * q + j
                m1[k, 0:R, :] = state[j * R : (j + 1) * R, :].astype(BF)
                both = [hf[h0:], hf[:h0], lf[h0:], lf[:h0]] if h0 else [hf, lf]
                m1[k, R : R + 16, :] = jnp.concatenate(both, axis=0).astype(BF)

                @pl.when(k != me)
                def _():
                    first(k).start()

                @pl.when(k == me)
                def _():
                    i1[k] = m1[k]

        group_row = lax.broadcasted_iota(jnp.int32, (8, LANES), 0)
        group_lane = lax.broadcasted_iota(jnp.int32, (8, LANES), 1) // span

        def join():
            def wait(k):
                @pl.when(k != me)
                def _():
                    first_wait(k).wait()

            loop(n, wait)

            def one(step):
                j = n - 1 - step if reverse else step
                tail = i1[j, R : R + 16, :].astype(F32)
                decay = tail[0:8] + tail[8:16]
                now = a.joined[step % 2 if isinstance(step, int) else lax.rem(step, 2)]
                means = [jnp.mean(now[g * span : (g + 1) * span], axis=0, keepdims=True) for g in range(groups)]
                means = jnp.concatenate(means + [jnp.zeros((8 - groups, LANES), F32)], axis=0)
                size = jnp.sum(means * means, axis=1, keepdims=True) + 1e-30
                along = nt(means.astype(BF), now.astype(BF)) / size
                along = jnp.where(group_row == group_lane, along, 0.0)
                ah, mh = along.astype(BF).astype(F32), means.astype(BF).astype(F32)
                al, ml = (along - ah).astype(BF).astype(F32), (means - mh).astype(BF).astype(F32)
                left, right = [], []
                for g in range(groups):
                    row = slice(g, g + 1)
                    left += [ah[row], ah[row], al[row]]
                    right += [mh[row], ml[row], mh[row]]
                rest = [jnp.zeros((8 - 3 * groups, LANES), F32)]
                left, right = jnp.concatenate(left + rest, axis=0), jnp.concatenate(right + rest, axis=0)
                o2[j, 0:R, :] = (now - tn(left, right))[0:R].astype(BF)
                o2[j, R : R + 16, :] = jnp.concatenate([left, right], axis=0).astype(BF)
                after = [
                    decay[g : g + 1, :] * now[g * span : (g + 1) * span]
                    + i1[j, g * span : (g + 1) * span, :].astype(F32)
                    for g in range(groups)
                ]
                if R < LANES:
                    after.append(jnp.zeros((LANES - R, N), F32))
                a.joined[(step + 1) % 2 if isinstance(step, int) else lax.rem(step + 1, 2)] = jnp.concatenate(after, axis=0)

                @pl.when((j != me) & (j != none))
                def _():
                    second(j).start()

                @pl.when((j == me) & (j != none))
                def _():
                    i2[j] = o2[j]

            a.joined[0] = jnp.zeros((LANES, N), F32)
            if n <= 8:
                for step in range(n):
                    one(step)
            else:
                loop(n, one)

        def collect(out, base):
            def wait(k):
                @pl.when((k != me) & (me != none))
                def _():
                    second_wait(k).wait_recv()

                @pl.when((k != me) & (k != none))
                def _():
                    second_wait(k).wait_send()

            loop(n, wait)

            @pl.when(me != none)
            def _():
                def one(k):
                    tail = i2[k, R : R + 16, :].astype(F32)
                    got = i2[k, 0:R, :].astype(F32) + tn(tail[0:8], tail[8:16])[0:R]
                    out[pl.ds(pl.multiple_of(base + k * R, 16), R), :] = got

                if n <= 8:
                    for k in range(n):
                        one(k)
                else:
                    loop(n, one)

            @pl.when(me == none)
            def _():
                out[base : base + Sh * C, :] = jnp.zeros((Sh * C, N), F32)

        return pack, join, collect

    forward = [states("f" + x, False) for x in "01"]
    backward = [states("b" + x, True) for x in "01"]

    def scan_inputs(s, i, pack):
        for c in range(0, C, LANES):
            v, d = conv(a.vext, a.conv_value, a.conv_value_bias, s, c)
            a.V[s, :, c : c + LANES] = v.astype(BF)
            a.dsv[s, :, c : c + LANES] = d.astype(BF)
        for c in range(0, 2 * N, LANES):
            v, d = conv(a.sext, a.conv_shared, a.conv_shared_bias, s, c)
            a.KR[s, :, c : c + LANES] = v.astype(BF)
            a.dss[s, :, c : c + LANES] = d.astype(BF)
        raw = a.raw[s]
        steps = jnp.maximum(raw, 0.0) + jnp.log1p(jnp.exp(-jnp.abs(raw)))
        a.steps[s] = steps
        cum = mm_exact_left(a.tri[...], -steps * rate_row)
        a.cum[s] = cum
        cumT = cum.T[0:8]
        a.cumT[s] = cumT
        last = cum[T - 1 : T, :]
        tail = jnp.exp(last - cum)
        V = a.V[s].astype(F32)
        a.U[s] = (expand(steps) * V).astype(BF)
        tU = (expand(steps * tail) * V).astype(BF)
        a.tU[s] = tU
        state = tn(tU, a.KR[s, :, 0:N])
        a.sp[pl.ds(pl.multiple_of(s * C, C), C), :] = state
        decay = jnp.broadcast_to(jnp.exp(cumT[:, T - 1 : T]), (8, LANES))
        a.decay[s] = decay
        pack(i, state, decay)

    def scan_half(which):
        loop(Sh, lambda i: scan_inputs(which * Sh + i, i, forward[which][0]))

    scan_half(0)
    loop(4 * Sh, lambda b: norm_block(4 * Sh + b))
    half(1, project_b)
    scan_half(1)

    def project_gate(s):
        a.gate[s] = mm(a.normed[s], a.gate_weight[...])

    def intra_forward(s):
        K, Rm = a.KR[s, :, 0:N], a.KR[s, :, N : 2 * N]
        G = jnp.where(rows_i >= cols_i, nt(Rm, K), 0.0)
        for p in range(H // 2):
            pair = slice(p * LANES, (p + 1) * LANES)
            U2 = a.U[s, :, pair]
            z = []
            for h in (2 * p, 2 * p + 1):
                gap = a.cum[s, :, h : h + 1] - a.cumT[s, h : h + 1, :]
                M = (jnp.exp(jnp.minimum(gap, 0.0)) * G).astype(BF)
                z.append(mm(M, U2))
            a.Y[s, :, pair] = jnp.where(first_half, z[0], z[1])

    loop(S, project_gate)
    half(0, intra_forward)
    forward[0][1]()
    half(1, intra_forward)

    cot_x.wait()
    cot_f = cot_copy(a.cotf.at[flip(head, 2)], flip(head, 2), 3, core_peer)
    cot_f.start()
    cot_c.wait()
    cot_f.wait()
    cot_own.wait()

    def back_out(s):
        total = nt(a.cotf[0, s], a.output_weight[:, 0:F])
        for f in range(1, D // F):
            total = total + nt(a.cotf[f, s], a.output_weight[:, f * F : (f + 1) * F])
        a.dext[s, 0:T, :] = total

    loop(S, back_out)
    forward[1][1]()

    def transposed(s):
        rows = pl.ds(pl.multiple_of(s * T, T), T)
        for c in range(0, D, 256):
            a.normT[c : c + 256, rows] = a.normed[s, :, c : c + 256].T

    loop(S, transposed)

    def outputs(s, i, stat):
        rows = pl.ds(pl.multiple_of(s * C, C), C)
        high, low = split(a.Sin[rows, :])
        Rm = a.KR[s, :, N : 2 * N]
        reach = expand(jnp.exp(a.cum[s]))
        outer = reach * (nt(Rm, high) + nt(Rm, low))
        Y = a.Y[s] + outer + skip_row * a.V[s].astype(F32)
        a.Y[s] = Y
        g = a.gate[s]
        gated = Y * (g * sigmoid(g))
        dots = a.dext[s, 0:T, :] * a.out_gain[...] * gated
        ones = jnp.ones((8, C), BF)
        sq = nt(ones, (gated * gated).astype(BF))
        dt = nt(ones, dots.astype(BF))
        row8 = lax.broadcasted_iota(jnp.int32, (8, T), 0)
        part = jnp.where(row8 == 2 * i, sq, 0.0) + jnp.where(row8 == 2 * i + 1, dt, 0.0)
        stat[...] = part + jnp.where(row8 < 2 * i, stat[...], 0.0)

    def head_sums(stat, inbox, first):
        return [
            pltpu.make_async_remote_copy(
                src_ref=stat,
                dst_ref=inbox.at[i],
                send_sem=a.ssem.at[first + i],
                recv_sem=a.rsem.at[first + i],
                device_id=peer,
                device_id_type=MESH,
            )
            for i, peer in enumerate((x_peer, diag, core_peer))
        ]

    stats = [head_sums(a.stat.at[w], a.stin.at[w], 9 + 3 * w) for w in range(2)]
    inner = C * lax.axis_size("head")

    def output_half(w):
        a.stat[w] = jnp.zeros((8, T), F32)
        loop(Sh, lambda i: outputs(w * Sh + i, i, a.stat.at[w]))
        for copy in stats[w]:
            copy.start()

    def stat_half(w):
        for copy in stats[w]:
            copy.wait()
        total = a.stat[w] + (a.stin[w, 0] + a.stin[w, 1]) + a.stin[w, 2]
        columns = []
        for i in range(Sh):
            scale = lax.rsqrt(total[2 * i : 2 * i + 1] / inner + EPSILON)
            columns += [scale, total[2 * i + 1 : 2 * i + 2] * scale / inner]
        stacked = jnp.concatenate(columns + [jnp.zeros((LANES - 2 * Sh, T), F32)], axis=0).T
        for i in range(Sh):
            a.gscale[i] = jnp.broadcast_to(stacked[:, 2 * i : 2 * i + 1], (T, LANES))
            a.gmean[i] = jnp.broadcast_to(stacked[:, 2 * i + 1 : 2 * i + 2], (T, LANES))

    def gate_back(s, i, pack):
        reach = expand(jnp.exp(a.cum[s]))
        scale, mean = a.gscale[i], a.gmean[i]
        cols = pl.ds(pl.multiple_of(s * T, T), T)
        for c in range(0, C, LANES):
            ch = slice(c, c + LANES)
            g, Y = a.gate[s, :, ch], a.Y[s, :, ch]
            sig = sigmoid(g)
            act = g * sig
            gu = Y * act * scale
            og = a.out_gain[0:1, ch]
            ny = gu * og
            a.ny[s, :, ch] = ny.astype(BF)
            a.nyT[ch, cols] = ny.T.astype(BF)
            dn = a.dext[s, 0:T, ch]
            a.small[5:6, ch] += jnp.sum(dn * gu, axis=0, keepdims=True)
            dg = scale * (dn * og - gu * mean)
            dY = (dg * act).astype(BF)
            a.dY[s, :, ch] = dY
            a.ecdY[s, :, ch] = (reach[:, ch] * dY.astype(F32)).astype(BF)
            a.normed[s, :, ch] = (dg * Y * sig * (1.0 + g * (1.0 - sig))).astype(BF)
        state = tn(a.ecdY[s], a.KR[s, :, N : 2 * N])
        pack(i, state, a.decay[s])

    for w in range(2):
        forward[w][2](a.Sin, w * Sh * C)
        output_half(w)
    for w in range(2):
        stat_half(w)
        loop(Sh, lambda i: gate_back(w * Sh + i, i, backward[w][0]))

    levels = []
    bit = 1
    while bit < n:
        levels.append(((flip(me, bit), head), lax.rem(me // bit, 2)))
        bit *= 2
    L = len(levels)
    sems = (a.asend, a.arecv, a.afree)
    head_levels = [(core_peer, lax.rem(head, 2)), (x_peer, lax.rem(head // 2, 2))]
    tasks, used = {}, 0
    for name, buf, inbox, count, order in (
        ("O", a.gwo, a.gwo_in, 2, levels),
        ("G", a.gwg, a.gwg_in, 2, levels),
        ("V", a.gwv, a.gwv_in, 4, levels),
        ("S", a.gws, a.gws_in, 1, head_levels + levels),
    ):
        rows = buf.shape[0] // count
        for c in range(count):
            inbase = c * inbox_rows(rows, len(order))
            red = Reduced(buf, c * rows, rows, inbox, inbase, order, sems, used)
            tasks[name + str(c)] = red.steps()
            used += 2 * len(order)

    def pump(*names):
        for name in names:
            next(tasks[name], None)

    def feature_sum(tag, block):
        sb1, sb2 = a.sb1, a.sb2
        rb1, rb2 = (a.__dict__[k + tag] for k in ("rb1", "rb2"))
        sem = a.__dict__["fsem" + tag]

        def copy1(s):
            return pltpu.make_async_remote_copy(
                src_ref=sb1.at[s],
                dst_ref=rb1.at[s],
                send_sem=sem.at[0, s],
                recv_sem=sem.at[1, s],
                device_id=core_peer,
                device_id_type=MESH,
            )

        def copy2(s):
            return pltpu.make_async_remote_copy(
                src_ref=sb2.at[s],
                dst_ref=rb2.at[s],
                send_sem=sem.at[2, s],
                recv_sem=sem.at[3, s],
                device_id=x_peer,
                device_id_type=MESH,
            )

        def one(s):
            sb1[s, 0] = block(s, flip(head, 1)).astype(BF)
            sb1[s, 1] = block(s, flip(flip(head, 1), 2)).astype(BF)
            copy1(s).start()

        def two(s):
            far = block(s, flip(head, 2))
            copy1(s).wait()
            sb2[s] = (far + rb1[s, 1].astype(F32)).astype(BF)
            copy2(s).start()

        def three(s):
            near = block(s, head)
            copy2(s).wait()
            return near + rb1[s, 0].astype(F32) + rb2[s].astype(F32)

        return one, two, three

    def features(f):
        return pl.ds(pl.multiple_of(f * F, F), F)

    o_one, o_two, o_three = feature_sum("o", lambda s, f: mm(a.ny[s], a.output_weight[:, features(f)]))

    def grad_out_weight(half_index):
        for g in range(D // F // 2):
            f = half_index * (D // F // 2) + g
            x = mm(a.nyT[...], a.cotf[f].reshape(S * T, F))
            a.gwo[half_index * C : (half_index + 1) * C, g * F : (g + 1) * F] = x.astype(BF)

    def weight_grad(out, r, rows, columns):
        out[r : r + rows, :] = mm(a.normT[r : r + rows, :], columns()).astype(BF)

    grad_out_weight(0)
    pump("O0")
    grad_out_weight(1)
    pump("O1")
    backward[0][1]()
    loop(S, o_one)
    weight_grad(a.gwg, 0, D // 2, lambda: a.normed[:, :, 0:C].reshape(S * T, C))
    pump("G0")
    weight_grad(a.gwg, D // 2, D // 2, lambda: a.normed[:, :, 0:C].reshape(S * T, C))
    backward[1][1]()
    pump("O0", "G1")
    loop(S, o_two)
    pump("O1")

    def intra_backward(s):
        K, Rm = a.KR[s, :, 0:N], a.KR[s, :, N : 2 * N]
        GT = jnp.where(rows_i <= cols_i, nt(K, Rm), 0.0)
        dGT = jnp.zeros((T, T), F32)
        for p in range(H // 2):
            pair = slice(p * LANES, (p + 1) * LANES)
            dY2, U2 = a.dY[s, :, pair], a.U[s, :, pair]
            z = []
            for h in (2 * p, 2 * p + 1):
                gap = a.cumT[s, h : h + 1, :] - a.cum[s, :, h : h + 1]
                LT = jnp.exp(jnp.minimum(gap, 0.0))
                mine = first_half if h == 2 * p else jnp.logical_not(first_half)
                Um = jnp.where(mine, U2.astype(F32), 0.0).astype(BF)
                dGT = dGT + nt(Um, dY2) * LT
                z.append(mm((LT * GT).astype(BF), dY2))
            a.dext[s, 0:T, pair] = jnp.where(first_half, z[0], z[1])
        a.dGT[s] = jnp.where(rows_i <= cols_i, dGT, 0.0).astype(BF)

    def out_rows(s):
        total = o_three(s)
        own = a.tokens[s, :, features(head)].astype(F32)
        a.mixed[s] = (own + total).astype(BF)

    half(0, intra_backward)
    pump("O0", "O1")
    half(1, intra_backward)
    pump("G0", "O0", "O1")
    loop(S, out_rows)
    pump("G1", "O0")

    def state_back(s):
        rows = pl.ds(pl.multiple_of(s * C, C), C)
        K, Rm = a.KR[s, :, 0:N], a.KR[s, :, N : 2 * N]
        gout, Sin = a.gout[rows, :], a.Sin[rows, :]
        gob = gout.astype(BF)
        cum, steps = a.cum[s], a.steps[s]
        tail = expand(jnp.exp(cum[T - 1 : T, :] - cum))
        V = a.V[s].astype(F32)
        dY = a.dY[s].astype(F32)
        dU = a.dext[s, 0:T, :] + tail * nt(K, gob)
        skipV = skip_row * V
        dV = expand(steps) * dU + skip_row * dY
        a.small[6:7, :] += jnp.sum(dY * V, axis=0, keepdims=True)
        ph, plo = split(dU * V)
        dsd = mm(ph, a.ET[...]) + mm(plo, a.ET[...])
        ph, plo = split(dY * (a.Y[s] - skipV))
        row = mm(ph, a.ET[...]) + mm(plo, a.ET[...])
        dcv = dV * a.dsv[s].astype(F32)
        a.dext[s, 0:T, :] = dcv
        dGT = a.dGT[s]
        sh, sl = split(Sin)
        dK = mm(dGT, Rm) + mm(a.tU[s], gob)
        dR = tn(dGT, K) + (mm(a.ecdY[s], sh) + mm(a.ecdY[s], sl))
        a.dsext[s, 0:T, 0:N] = dK * a.dss[s, :, 0:N].astype(F32)
        a.dsext[s, 0:T, N : 2 * N] = dR * a.dss[s, :, N : 2 * N].astype(F32)
        decay = a.decay[s]
        sums = []
        for h in range(H):
            hs = slice(h * PW, (h + 1) * PW)
            sp = a.sp[pl.ds(pl.multiple_of(s * C + h * PW, PW), PW), :]
            sums.append(jnp.sum(gout[hs] * (decay[h : h + 1] * Sin[hs] + sp), axis=0, keepdims=True))
        sums = jnp.concatenate(sums + [jnp.zeros((LANES - H, LANES), F32)], axis=0)
        ones = jnp.ones((8, LANES), BF)
        lh, ll = split(sums)
        end = (nt(ones, lh) + nt(ones, ll))[0:1]
        dld = mm_exact_left(a.triT[...], row - steps * dsd) + end
        draw = (dsd - rate_row * dld) * sigmoid(a.raw[s])
        a.heads_sm[0:1, :] += jnp.sum(draw, axis=0, keepdims=True)
        a.heads_sm[1:2, :] -= jnp.sum(steps * dld, axis=0, keepdims=True)
        a.dst[s] = draw.astype(BF)
        a.dstT[:, pl.ds(pl.multiple_of(s * T, T), T)] = draw.T[0:16].astype(BF)

    backward[0][2](a.gout, 0)
    half(0, state_back)
    pump("O1", "G0", "G1")
    backward[1][2](a.gout, Sh * C)
    half(1, state_back)
    a.stepsum[...] = nt(a.dstT[...], a.normT[...])[0:8]

    def edge_copy(src, dst, sem):
        return pltpu.make_async_remote_copy(
            src_ref=src.at[:, pl.ds(0, 8), :],
            dst_ref=dst,
            send_sem=a.ssem.at[sem],
            recv_sem=a.rsem.at[sem],
            device_id=(lax.rem(me + n - 1, n), head),
            device_id_type=MESH,
        )

    edges = [edge_copy(a.dext, a.ev, 7), edge_copy(a.dsext, a.es, 8)]

    @pl.when(me > 0)
    def _():
        for copy in edges:
            copy.start()

    pump("O0", "G0", "G1")

    def conv_grads(s):
        for ext, grad, out, base, width in (
            (a.vext, a.dext, a.small, 0, C),
            (a.sext, a.dsext, a.shsm, 0, 2 * N),
        ):
            for c in range(0, width, LANES):
                ch = slice(c, c + LANES)
                d = grad[s, 0:T, ch]
                for k in range(4):
                    x = ext[s, pl.ds(5 + k, T), ch]
                    out[base + k : base + k + 1, ch] += jnp.sum(d * x, axis=0, keepdims=True)
                out[base + 4 : base + 5, ch] += jnp.sum(d, axis=0, keepdims=True)

    loop(S, conv_grads)
    a.pack[...] = jnp.zeros(a.pack.shape, F32)
    a.pack[0:7, 0:C] = a.small[0:7, :]
    a.pack[0:2, C : C + LANES] = a.heads_sm[0:2, :]
    a.pack[8:16, :] = a.stepsum[...]
    a.pack[16:21, 0 : 2 * N] = a.shsm[0:5, :]

    def whole_sum(buf, inbox, partners, first):
        for i, partner in enumerate(partners):
            copy = pltpu.make_async_remote_copy(
                src_ref=buf,
                dst_ref=inbox.at[i],
                send_sem=a.psend.at[first + i],
                recv_sem=a.precv.at[first + i],
                device_id=partner,
                device_id_type=MESH,
            )
            copy.start()
            yield
            copy.wait()
            buf[...] = buf[...] + inbox[i]

    def small_sums():
        partners = [partner for partner, _ in levels]
        yield from whole_sum(a.pack, a.packin, partners, 0)
        yield from whole_sum(a.pack.at[pl.ds(16, 8), :], a.shin, [x_peer, core_peer], L)

    tasks["P"] = small_sums()
    tasks["N"] = whole_sum(a.ngain, a.ngin, [partner for partner, _ in levels], L + 2)
    pump("P", "O1")

    @pl.when(me < n - 1)
    def _():
        for copy in edges:
            copy.wait_recv()
        for s in range(S):
            a.dext[s, T : T + 8, :] = a.ev[s]
            a.dsext[s, T : T + 8, :] = a.es[s]

    @pl.when(me == n - 1)
    def _():
        for s in range(S):
            a.dext[s, T : T + 8, :] = jnp.zeros((8, C), F32)
            a.dsext[s, T : T + 8, :] = jnp.zeros((8, 2 * N), F32)

    @pl.when(me > 0)
    def _():
        for copy in edges:
            copy.wait_send()

    def conv_back(s):
        for grad, w, out, shift, width in (
            (a.dext, a.conv_value, a.normed, C, C),
            (a.dsext, a.conv_shared, a.dsl, 0, 2 * N),
        ):
            for c in range(0, width, LANES):
                ch = slice(c, c + LANES)
                total = w[3:4, ch] * grad[s, 0:T, ch]
                for k in range(3):
                    total = total + w[k : k + 1, ch] * grad[s, pl.ds(3 - k, T), ch]
                out[s, :, shift + c : shift + c + LANES] = total.astype(BF)

    loop(S, conv_back)

    weight_grad(a.gws, 0, D, lambda: a.dsl[...].reshape(S * T, 2 * N))
    pump("S0")
    for c in range(4):
        weight_grad(a.gwv, c * D // 4, D // 4, lambda: a.normed[:, :, C : 2 * C].reshape(S * T, C))
        pump("V" + str(c))
        if c == 1:
            pump("S0", "P")
    pump("O0", "O1", "G0", "G1")

    def d_normed(s, f):
        rows = features(f)
        return (
            nt(a.normed[s, :, 0:C], a.gate_weight[rows, :])
            + nt(a.normed[s, :, C : 2 * C], a.value_weight[rows, :])
            + nt(a.dsl[s], a.shared_weight[rows, :])
            + mm(a.dst[s], a.stT[:, rows])
        )

    d_one, d_two, d_three = feature_sum("d", d_normed)
    half(0, d_one)
    pump("V0", "S0", "P")
    half(1, d_one)
    pump("V1", "V0", "O1", "S0")
    half(0, d_two)
    pump("V2", "V1", "V0", "P")
    half(1, d_two)
    pump("V3", "V2", "V1", "V0", "S0", "P")

    own_gain = a.norm_gain[0:1, features(head)]

    def feature_rows(s):
        d = d_three(s)
        a.dfeat[s] = d
        unit = a.tokens[s, :, features(head)].astype(F32) * a.rms[s][:, 0:1]
        a.ngain[0:1, :] += jnp.sum(d * unit, axis=0, keepdims=True)
        ones = jnp.ones((8, F), BF)
        dh, dl = split(d * own_gain * unit)
        dot = nt(ones, dh) + nt(ones, dl)
        row8 = lax.broadcasted_iota(jnp.int32, (8, T), 0)
        a.stat2[...] = jnp.where(row8 == s, dot, 0.0) + jnp.where(row8 < s, a.stat2[...], 0.0)

    a.ngain[...] = jnp.zeros(a.ngain.shape, F32)
    a.stat2[...] = jnp.zeros(a.stat2.shape, F32)
    half(0, feature_rows)
    pump("V3", "V2", "V1", "S0")
    half(1, feature_rows)
    stats2 = head_sums(a.stat2, a.stin2, 15)
    for copy in stats2:
        copy.start()
    pump("N", "V3", "V2", "P", "V0", "S0")
    for copy in stats2:
        copy.wait()
    total2 = a.stat2[...] + (a.stin2[0] + a.stin2[1]) + a.stin2[2]
    cols2 = jnp.concatenate([total2 / D, jnp.zeros((LANES - 8, T), F32)], axis=0).T
    for s in range(S):
        unit = a.tokens[s, :, features(head)].astype(F32) * a.rms[s][:, 0:1]
        inner_part = a.dfeat[s] * own_gain - unit * cols2[:, s : s + 1]
        a.gtok[s] = a.cotangent[s].astype(F32) + a.rms[s][:, 0:1] * inner_part
    order = ("N", "V3", "V1", "V0", "S0", "P", "O0", "O1", "G0", "G1", "V2")
    for _ in range(4 * (L + 3)):
        pump(*order)
    done = [
        pltpu.make_async_copy(a.gwo, a.out_gwo, a.lsem.at[1]),
        pltpu.make_async_copy(a.gwg, a.out_gwg, a.lsem.at[2]),
        pltpu.make_async_copy(a.gwv, a.out_gwv, a.lsem.at[3]),
        pltpu.make_async_copy(a.gws, a.out_gws, a.lsem.at[4]),
    ]
    for copy in done:
        copy.start()
    a.o_small[...] = a.pack[...]
    a.o_ngain[...] = a.ngain[...]
    for copy in done:
        copy.wait()


INPUTS = [
    "tokens",
    "norm_gain",
    "gate_weight",
    "value_weight",
    "shared_weight",
    "step_weight",
    "conv_value",
    "conv_value_bias",
    "conv_shared",
    "conv_shared_bias",
    "step_bias",
    "decay_rate",
    "skip_weight",
    "out_gain",
    "output_weight",
    "cotangent",
]
OUTPUTS = ["mixed", "gtok", "out_gwg", "out_gwv", "out_gws", "out_gwo", "o_small", "o_ngain"]


def inbox_rows(size, count):
    total = 0
    for _ in range(count):
        size = size // 2 if size // 2 >= 16 else size
        total += size
    return total


def scratch(dims):
    n, S, T, D, C, H, N, F = dims
    R = S // 2 * C // n
    L = n.bit_length() - 1
    vm = pltpu.VMEM
    dma = pltpu.SemaphoreType.DMA
    items = dict(
        tri=vm((T, T), BF),
        triT=vm((T, T), BF),
        E2=vm((2 * LANES, C), BF),
        ET=vm((C, LANES), BF),
        stT=vm((LANES, D), BF),
        skipE=vm((8, C), F32),
        hrow=vm((8, LANES), F32),
        small=vm((8, C), F32),
        heads_sm=vm((8, LANES), F32),
        shsm=vm((8, 2 * N), F32),
        normed=vm((S, T, D), BF),
        normT=vm((D, S * T), BF),
        rms=vm((S, T, LANES), F32),
        halo=vm((S, 16, D), BF),
        cotf=vm((D // F, S, T, F), BF),
        vext=vm((S, T + 8, C), F32),
        sext=vm((S, T + 8, 2 * N), F32),
        raw=vm((S, T, LANES), F32),
        steps=vm((S, T, LANES), F32),
        cum=vm((S, T, LANES), F32),
        cumT=vm((S, 8, T), F32),
        decay=vm((S, 8, LANES), F32),
        V=vm((S, T, C), BF),
        KR=vm((S, T, 2 * N), BF),
        dsv=vm((S, T, C), BF),
        dss=vm((S, T, 2 * N), BF),
        U=vm((S, T, C), BF),
        tU=vm((S, T, C), BF),
        sp=vm((S * C, N), F32),
        Sin=vm((S * C, N), F32),
        gout=vm((S * C, N), F32),
        joined=vm((2, LANES, N), F32),
        gate=vm((S, T, C), F32),
        Y=vm((S, T, C), F32),
        stat=vm((2, 8, T), F32),
        stin=vm((2, 3, 8, T), F32),
        stat2=vm((8, T), F32),
        stin2=vm((3, 8, T), F32),
        gscale=vm((S // 2, T, LANES), F32),
        gmean=vm((S // 2, T, LANES), F32),
        ny=vm((S, T, C), BF),
        nyT=vm((C, S * T), BF),
        dY=vm((S, T, C), BF),
        ecdY=vm((S, T, C), BF),
        dGT=vm((S, T, T), BF),
        dext=vm((S, T + 8, C), F32),
        dsext=vm((S, T + 8, 2 * N), F32),
        ev=vm((S, 8, C), F32),
        es=vm((S, 8, 2 * N), F32),
        dsl=vm((S, T, 2 * N), BF),
        dst=vm((S, T, LANES), BF),
        dstT=vm((16, S * T), BF),
        stepsum=vm((8, D), F32),
        gwo=vm((2 * C, D // 2), BF),
        gwo_in=vm((2 * inbox_rows(C, L), D // 2), BF),
        gwg=vm((D, C), BF),
        gwg_in=vm((2 * inbox_rows(D // 2, L), C), BF),
        gwv=vm((D, C), BF),
        gwv_in=vm((4 * inbox_rows(D // 4, L), C), BF),
        gws=vm((D, 2 * N), BF),
        gws_in=vm((inbox_rows(D, L + 2), 2 * N), BF),
        dfeat=vm((S, T, F), F32),
        ngain=vm((8, F), F32),
        pack=vm((24, D), F32),
        packin=vm((L, 24, D), F32),
        shin=vm((2, 8, D), F32),
        ngin=vm((L, 8, F), F32),
        ssem=dma((18,)),
        rsem=dma((18,)),
        lsem=dma((5,)),
        asend=dma((16 * L + 2 * (L + 2),)),
        arecv=dma((16 * L + 2 * (L + 2),)),
        afree=pltpu.SemaphoreType.REGULAR((16 * L + 2 * (L + 2),)),
        psend=dma((2 * L + 2,)),
        precv=dma((2 * L + 2,)),
    )
    for key in ("m10", "m11", "o20", "o21"):
        items[key] = vm((n, R + 16, N), BF)
    items["sb1"] = vm((S, 2, T, F), BF)
    items["sb2"] = vm((S, T, F), BF)
    for tag in ("f0", "f1", "b0", "b1"):
        for key in ("i1", "i2"):
            items[key + tag] = vm((n, R + 16, N), BF)
        for key in ("s1", "r1", "s2", "r2"):
            items[key + tag] = dma((n,))
    for tag in "od":
        items["rb1" + tag] = vm((S, 2, T, F), BF)
        items["rb2" + tag] = vm((S, T, F), BF)
        items["fsem" + tag] = dma((4, S))
    return items


def dims_names(dims):
    return INPUTS + OUTPUTS + list(scratch(dims))


def finish(dims, mixed, gtok, gwg, gwv, gws, left, right, small, ngain, *outs):
    n, S, T, D, C, H, N, F = dims
    PW = C // H
    outs[0][...] = mixed[...]
    outs[1][...] = gtok[...]
    outs[3][...] = gwg[...].astype(F32)
    outs[4][...] = gwv[...].astype(F32)
    outs[5][...] = gws[...].astype(F32)
    outs[15][:, 0 : D // 2] = left[...].astype(F32)
    outs[15][:, D // 2 : D] = right[...].astype(F32)

    @pl.when(pl.program_id(0) == 0)
    def _():
        outs[2][...] = ngain[0:1, :]
        outs[6][...] = small[8 : 8 + H, :]
        outs[7][...] = small[0:4, 0:C]
        outs[8][...] = small[4:5, 0:C]
        outs[9][...] = small[16:20, 0 : 2 * N]
        outs[10][...] = small[20:21, 0 : 2 * N]
        outs[11][...] = small[0:1, C : C + H]
        outs[12][...] = small[1:2, C : C + H]
        sums = [jnp.sum(small[6:7, h * PW : (h + 1) * PW], axis=1, keepdims=True) for h in range(H)]
        outs[13][...] = jnp.concatenate(sums, axis=1)
        outs[14][...] = small[5:6, 0:C]


def shards(*args):
    tokens, gate_weight, step_weight, shared_weight = args[0], args[2], args[5], args[4]
    cotangent = args[15]
    S, T, D = tokens.shape
    C, H, N, F = gate_weight.shape[1], step_weight.shape[1], shared_weight.shape[1] // 2, cotangent.shape[2]
    n = lax.axis_size("seq")
    dims = (n, S, T, D, C, H, N, F)
    args = [x.reshape(1, -1) if x.ndim == 1 else x for x in args]
    args[5] = step_weight.T
    items = scratch(dims)
    whole = pl.BlockSpec(memory_space=pltpu.VMEM)
    hbm = pl.BlockSpec(memory_space=pl.ANY)
    struct = jax.ShapeDtypeStruct
    mixed, gtok, gwg, gwv, gws, gwo, small, ngain = pl.pallas_call(
        lambda *refs: kernel(dims, *refs),
        out_shape=(
            struct((S, T, F), BF),
            struct((S, T, F), F32),
            struct((D, C), BF),
            struct((D, C), BF),
            struct((D, 2 * N), BF),
            struct((2 * C, D // 2), BF),
            struct((24, D), F32),
            struct((8, F), F32),
        ),
        in_specs=[whole] * len(args),
        out_specs=(whole, whole, hbm, hbm, hbm, hbm, whole, whole),
        scratch_shapes=list(items.values()),
        compiler_params=pltpu.CompilerParams(
            collective_id=0, has_side_effects=True, vmem_limit_bytes=63 * 2**20
        ),
        name="block",
    )(*args)
    outs = pl.pallas_call(
        lambda *refs: finish(dims, *refs),
        grid=(S,),
        out_shape=(
            struct((S, T, F), BF),
            struct((S, T, F), F32),
            struct((1, F), F32),
            struct((D, C), F32),
            struct((D, C), F32),
            struct((D, 2 * N), F32),
            struct((H, D), F32),
            struct((4, C), F32),
            struct((1, C), F32),
            struct((4, 2 * N), F32),
            struct((1, 2 * N), F32),
            struct((1, H), F32),
            struct((1, H), F32),
            struct((1, H), F32),
            struct((1, C), F32),
            struct((C, D), F32),
        ),
        in_specs=[
            pl.BlockSpec((1, T, F), lambda i: (i, 0, 0)),
            pl.BlockSpec((1, T, F), lambda i: (i, 0, 0)),
            pl.BlockSpec((D // S, C), lambda i: (i, 0)),
            pl.BlockSpec((D // S, C), lambda i: (i, 0)),
            pl.BlockSpec((D // S, 2 * N), lambda i: (i, 0)),
            pl.BlockSpec((C // S, D // 2), lambda i: (i, 0)),
            pl.BlockSpec((C // S, D // 2), lambda i: (i + S, 0)),
            pl.BlockSpec((24, D), lambda i: (0, 0)),
            pl.BlockSpec((8, F), lambda i: (0, 0)),
        ],
        out_specs=(
            pl.BlockSpec((1, T, F), lambda i: (i, 0, 0)),
            pl.BlockSpec((1, T, F), lambda i: (i, 0, 0)),
            pl.BlockSpec((1, F), lambda i: (0, 0)),
            pl.BlockSpec((D // S, C), lambda i: (i, 0)),
            pl.BlockSpec((D // S, C), lambda i: (i, 0)),
            pl.BlockSpec((D // S, 2 * N), lambda i: (i, 0)),
            pl.BlockSpec((H, D), lambda i: (0, 0)),
            pl.BlockSpec((4, C), lambda i: (0, 0)),
            pl.BlockSpec((1, C), lambda i: (0, 0)),
            pl.BlockSpec((4, 2 * N), lambda i: (0, 0)),
            pl.BlockSpec((1, 2 * N), lambda i: (0, 0)),
            pl.BlockSpec((1, H), lambda i: (0, 0)),
            pl.BlockSpec((1, H), lambda i: (0, 0)),
            pl.BlockSpec((1, H), lambda i: (0, 0)),
            pl.BlockSpec((1, C), lambda i: (0, 0)),
            pl.BlockSpec((C // S, D), lambda i: (i, 0)),
        ),
        name="finish",
    )(mixed, gtok, gwg, gwv, gws, gwo, gwo, small, ngain)
    outs = list(outs)
    outs[6] = outs[6].T
    for i in (2, 8, 10, 11, 12, 13, 14):
        outs[i] = outs[i].reshape(-1)
    return tuple(outs)


def solution(mesh):
    head = P("head")
    return jax.shard_map(
        shards,
        mesh=mesh,
        in_specs=(
            P(None, "seq", None),
            P(),
            P(None, "head"),
            P(None, "head"),
            P(),
            P(None, "head"),
            P(None, "head"),
            head,
            P(),
            P(),
            head,
            head,
            head,
            head,
            P("head", None),
            P(None, "seq", "head"),
        ),
        out_specs=(
            P(None, "seq", "head"),
            P(None, "seq", "head"),
            head,
            P(None, "head"),
            P(None, "head"),
            P(),
            P(None, "head"),
            P(None, "head"),
            head,
            P(),
            P(),
            head,
            head,
            head,
            head,
            P("head", None),
        ),
        check_vma=False,
    )
```

time: 732 us -> 182 us (0.25); the launches traced: 723 us -> 182 us
  waiting for transfers between devices: 363 us -> 0 us
  Pallas kernels: 0 us -> 181 us
  blocking collectives: 125 us -> 0 us
  matrix products: 101 us -> 0 us
  other arithmetic: 65.6 us -> 0 us
  local copies, waits for them, and re-layouts: 39.5 us -> 0 us
  between operations: 15.5 us -> 0.84 us
  starting transfers between devices: 12.6 us -> 0 us
    psum x2 -> x0, waiting for transfers between devices: 274 us -> none  [the longest x1 218 us: shards(): summed = lax.psum(pending, 'seq')]
    pallas_call x0 -> x2, Pallas kernels: none -> 181 us  [the longest x1 174 us: shards(): pl.pallas_call(lambda *refs: kernel(dims, *refs), out_shape=(struct((S, T...]
    dot_general x27 -> x0, matrix products: 101 us -> none  [the longest x3 30.1 us: local_scan(): jnp.einsum('shtu,suhp->sthp', weights, values, precision=FULL_PRECISION)]
    psum x5 -> x0, blocking collectives: 98.6 us -> none  [the longest x1 42.9 us: shards(): lax.psum((grad_w_shared, grad_conv_shared, grad_conv_shared_bias), ('seq'...]
    all_gather x3 -> x0, waiting for transfers between devices: 88.3 us -> none  [the longest x1 47.2 us: carried_in_2(): lax.all_gather(part.astype(kind), axis)]
    all_gather x1 -> x0, blocking collectives: 26.3 us -> none  [carried_in(): lax.all_gather(a.astype(kind), axis)]
    reduce_sum x10 -> x0, other arithmetic: 22.1 us -> none  [the longest x2 6.63 us: conv_apply(): weight_matrix[offset] * extended[:, offset:offset + seq_rows, :]]
    unnamed x147 -> x0, local copies, waits for them, and re-layouts: 14.4 us -> none
  transfers between devices with their start and end apart: 11 -> 0, of which waited for: 4 -> 0; matrix products, arithmetic and copies ran while one was open for 22% -> 0% of each run, Pallas kernels for 0% -> 0%
where the time goes in v1:
time: 182 us
  Pallas kernels  181 us (99%)
    pallas_call x1, Pallas kernels, shards(): pl.pallas_call(lambda *refs: kernel(dims, *refs), out_shape=(struct((S, T...  174 us
    pallas_call x1, Pallas kernels, shards(): pl.pallas_call(lambda *refs: finish(dims, *refs), grid=(S,), out_shape=(s...  6.74 us

profile of v1, /device:TPU:0, one launch (start us, length us, event | category | flops | bytes accessed | tf_op | source)
XLA Modules:
  0.0 181.9 jit_solution(15354103068543342362)
XLA Ops:
  0.7 174.3 %block.1 = (bf16[4,256,256]{2,1,0:T(8,128)(2,1)}, f32[4,256,256]{2,1,0:T(8,128)}, bf16[1024,512]{1,0:T(8,128)(2,1)}, bf16[1024,512]{1,0:T(8,128)(2,1)}, bf16[102...) custom-call(bf16[4,256,1024]{2,1,0:T(8,128)(2,1)} %refs_0_.1, ...), custom_call_target="tpu_custom_call" | custom-call | tf_op jit(solution)/shard_map/block/pallas_call | solution.py:1114
  174.9 6.7 %finish.1 = (bf16[4,256,256]{2,1,0:T(8,128)(2,1)}, f32[4,256,256]{2,1,0:T(8,128)}, f32[1,256]{1,0:T(1,128)}, f32[1024,512]{1,0:T(8,128)}, f32[1024,512]{1,0:T(8,...) custom-call(bf16[4,256,256]{2,1,0:T(8,128)(2,1)} %get-tuple-element., ...), custom_call_target="tpu_custom_call" | custom-call | tf_op jit(solution)/shard_map/finish/pallas_call | solution.py:1134
